TPU v7x, 512 devices: a whole 4x8x8 slice. The times are simulated.
512 devices in a mesh: tok: 32 (over z, x), cen: 16 (over y, core).
Axes of the slice: x: 4, y: 8, z: 8, core: 2. Of those that a mesh axis runs over, the one named last changes fastest.
Arguments:
- tokens: bfloat16 [4096, 128], P('tok'), may hold values from -128 to 128
- nearest: int32 [4096], P('tok'), may hold values from 0 to 524287
- centroids: bfloat16 [524288, 128], P(('tok', 'cen')), may hold values from -32 to 32
- log_prior: float32 [524288], P(('tok', 'cen')), may hold values from -1.2 to 3.4
Outputs:
- updated: bfloat16 [524288, 128], P(('tok', 'cen'))
- log_norm: float32 [4096], P('tok')
- residual: bfloat16 [4096, 128], P(('tok', 'cen'))
All inputs are finite; a program needn't handle non-finite values.
Results may differ from a plain program's by a relative error of at most 0.005.
Values may be sent and summed in bfloat16 or wider, within the bound.
A program may use at most 128 MiB of HBM per device.

v0:
```python
import math

import jax
import jax.numpy as jnp
from jax import lax
from jax.sharding import PartitionSpec as P


def local_scores(tblock, centroids, log_prior, scale):
    raw = lax.dot_general(
        tblock, centroids, (((1,), (1,)), ((), ())), preferred_element_type=jnp.float32
    )
    return raw * scale + log_prior[None, :]


def pick_rows(ids, first, centroids):
    local = centroids.shape[0]
    onehot = ((ids - first)[:, None] == jnp.arange(local, dtype=jnp.int32)[None, :]).astype(
        jnp.bfloat16
    )
    return jnp.dot(onehot, centroids, preferred_element_type=jnp.float32)


def per_device(tokens, nearest, centroids, log_prior):
    all_tok, all_ids = (
        lax.all_gather(tokens, "tok", axis=0, tiled=True),
        lax.all_gather(nearest, "tok", axis=0, tiled=True),
    )
    total = all_tok.shape[0]
    width = all_tok.shape[1]
    local = centroids.shape[0]
    scale = 1.0 / math.sqrt(width)
    block = min(512, total)
    count = total // block
    tok_blocks = all_tok.reshape(count, block, width)

    def first_pass(tblock):
        scores = local_scores(tblock, centroids, log_prior, scale)
        top = jnp.max(scores, axis=1)
        return (top, jnp.sum(jnp.exp(scores - top[:, None]), axis=1))

    part_max, part_sum = lax.map(first_pass, tok_blocks)
    part_max = part_max.reshape(total)
    part_sum = part_sum.reshape(total)
    whole_max = lax.pmax(part_max, ("tok", "cen"))
    whole_sum = lax.psum(part_sum * jnp.exp(part_max - whole_max), ("tok", "cen"))
    log_all = whole_max + jnp.log(whole_sum)

    def second_pass(carry, inputs):
        sums, mass = carry
        tblock, lblock = inputs
        scores = local_scores(tblock, centroids, log_prior, scale)
        weight = jnp.exp(scores - lblock[:, None]).astype(jnp.bfloat16)
        sums = sums + lax.dot_general(
            weight, tblock, (((0,), (0,)), ((), ())), preferred_element_type=jnp.float32
        )
        mass = mass + jnp.sum(weight.astype(jnp.float32), axis=0)
        return ((sums, mass), None)

    start = (jnp.zeros((local, width), jnp.float32), jnp.zeros((local,), jnp.float32))
    (sums, mass), unused = lax.scan(second_pass, start, (tok_blocks, log_all.reshape(count, block)))
    updated = (sums / mass[:, None]).astype(jnp.bfloat16)
    slab_rows = tokens.shape[0]
    log_norm = lax.dynamic_slice_in_dim(log_all, lax.axis_index("tok") * slab_rows, slab_rows)
    n_tok = lax.axis_size("tok")
    n_cen = lax.axis_size("cen")
    owned = total // (n_tok * n_cen)
    first = lax.axis_index(("tok", "cen")) * local
    picked = lax.psum_scatter(
        pick_rows(all_ids, first, centroids), ("tok", "cen"), scatter_dimension=0, tiled=True
    )
    mine = lax.dynamic_slice_in_dim(tokens, lax.axis_index("cen") * owned, owned)
    residual = (mine.astype(jnp.float32) - picked).astype(jnp.bfloat16)
    return (updated, log_norm, residual)


def solution(mesh):
    return jax.shard_map(
        per_device,
        mesh=mesh,
        in_specs=(P("tok", None), P("tok"), P(("tok", "cen"), None), P(("tok", "cen"))),
        out_specs=(P(("tok", "cen"), None), P("tok"), P(("tok", "cen"), None)),
        check_vma=False,
    )
```

profile of v0, /device:TPU:1, one launch (start us, length us, event | category | flops | bytes accessed | tf_op | source)
XLA Modules:
  0.0 580.6 jit_solution(1791176830207678930)
XLA Ops:
  8.0 36.5 %all-gather = s32[32,1,128]{2,1,0:T(1,128)S(1)} all-gather(s32[1,1,128]{2,1,0:T(1,128)} %bitcast.57), channel_id=1, replica_groups=mesh['tok'=32,'cen'=16] {'tok'}, dimensions={0}, use_global_device_ids=true | all-gather | bytes 16896 | tf_op jit(solution)/shard_map/all_gather | solution.py:27
  44.5 5.1 fusion.11
  49.7 0.5 all-gather.3.cloned.1.call-update
  50.3 286.8 %all-reduce.3.cloned.1.call-done = f32[4096,128]{1,0:T(8,128)} async-done(((f32[4096,128]{1,0:T(8,128)}), f32[4096,128]{1,0:T(8,128)}) %all-reduce.3.cloned.1.call-update) | async-done | bytes 2097168
  337.0 1.3 fusion.13
  338.3 17.3 %while.25 = (s32[]{:T(128)}, f32[8,512]{1,0:T(8,128)S(1)}, f32[8,512]{1,0:T(8,128)S(1)}, bf16[8,512,128]{2,1,0:T(8,128)(2,1)}, bf16[1024,128]{1,0:T(8,128)(2,1)S...) while((s32[]{:T(128)}, f32[8,512]{1,0:T(8,128)S(1)}, f32[8,512]{1,0:T(8,128)S(1)}, ...), condition=%wide.region_3.4_spmd, body=%wide.region_0.3_spmd.sunk | while | flops 137886720 | bytes 4610653 | solution.py:42
  338.3 1.4 fusion.24
  339.7 0.6 exponential_reduce_fusion.2
  340.4 0.1 dynamic_update_slice.9
  340.5 1.4 fusion.24
  341.9 0.6 exponential_reduce_fusion.2
  342.6 0.1 dynamic_update_slice.9
  342.6 1.4 fusion.24
  344.1 0.6 exponential_reduce_fusion.2
  344.7 0.1 dynamic_update_slice.9
  344.8 1.4 fusion.24
  346.2 0.6 exponential_reduce_fusion.2
  346.9 0.1 dynamic_update_slice.9
  347.0 1.4 fusion.24
  348.4 0.6 exponential_reduce_fusion.2
  349.1 1.4 fusion.24
  350.6 0.6 exponential_reduce_fusion.2
  351.3 1.4 fusion.24
  352.7 0.6 exponential_reduce_fusion.2
  353.5 1.4 fusion.24
  354.9 0.6 exponential_reduce_fusion.2
  355.5 0.1 dynamic_update_slice.9
  355.6 96.1 %pmax.7 = f32[4096]{0:T(1024)S(1)} all-reduce(f32[4096]{0:T(1024)S(1)} %bitcast.49), channel_id=1, replica_groups=mesh['tok'=32,'cen'=16] {'tok','cen'}, use_global_device_ids=true, to_apply=%region_4.5 | all-reduce | flops 4096 | bytes 32768 | tf_op jit(solution)/shard_map/pmax | solution.py:45
  451.8 94.9 %psum.7 = f32[4096]{0:T(1024)S(1)} all-reduce(f32[4096]{0:T(1024)S(1)} %exponential_multiply_fusion), channel_id=1, replica_groups=mesh['tok'=32,'cen'=16] {'tok','cen'}, use_global_device_ids=true, to_apply=%region_5.6 | all-reduce | flops 4096 | bytes 32768 | tf_op jit(solution)/shard_map/psum | solution.py:46
  546.7 25.0 %while.26 = (s32[]{:T(128)}, f32[1024,128]{1,0:T(8,128)S(1)}, f32[1024]{0:T(1024)S(1)}, bf16[8,512,128]{2,1,0:T(8,128)(2,1)}, bf16[1024,128]{1,0:T(8,128)(2,1)S(...) while((s32[]{:T(128)}, f32[1024,128]{1,0:T(8,128)S(1)}, ...), condition=%wide.region_8.9_spmd.clone, body=%wide.region_6.8_spmd.clone.sunk | while | flops 271844352 | bytes 3697772 | solution.py:61
  546.7 1.5 convert_reduce_fusion.2
  548.3 1.5 convolution_add_fusion.2
  549.8 1.5 convert_reduce_fusion.2
  551.4 1.5 convolution_add_fusion.2
  552.9 1.5 convert_reduce_fusion.2
  554.5 1.5 convolution_add_fusion.2
  556.1 1.5 convert_reduce_fusion.2
  557.6 1.5 convolution_add_fusion.2
  559.2 1.5 convert_reduce_fusion.2
  560.8 1.5 convolution_add_fusion.2
  562.3 1.5 convert_reduce_fusion.2
  563.9 1.5 convolution_add_fusion.2
  565.4 1.5 convert_reduce_fusion.2
  567.0 1.5 convolution_add_fusion.2
  568.6 1.5 convert_reduce_fusion.2
  570.1 1.5 convolution_add_fusion.2
  571.7 0.6 dynamic_slice.17
  572.3 0.9 divide_convert_fusion
  (45 shorter events, 0.9 us)
Async XLA Ops:
  8.0 329.0 %all-reduce.3.cloned.1.call-start = ((), (), s32[]{:S(2)}) async-start(), calls=%async_computation.1 | async-start | bytes 4194304
  49.6 288.7 %copy-start = (bf16[1024,128]{1,0:T(8,128)(2,1)S(1)}, bf16[1024,128]{1,0:T(8,128)(2,1)}, u32[]{:S(2)}) copy-start(bf16[1024,128]{1,0:T(8,128)(2,1)} %param.10) | copy-start | bytes 786436
  49.6 288.7 %copy-start.1 = (f32[1024]{0:T(1024)S(1)}, f32[1024]{0:T(1024)}, u32[]{:S(2)}) copy-start(f32[1024]{0:T(1024)} %param.11) | copy-start | bytes 12292
  49.6 288.7 %all-gather.3.cloned.1.call-start = ((), (), s32[]{:S(2)}) async-start(), calls=%async_computation | async-start | bytes 1081344 | tf_op jit(solution)/shard_map/all_gather | solution.py:26
Sparse Core Ops, SparseCore 0:
  49.7 287.2 all-reduce.2
Sparse Core Ops, SparseCore 1:
  53.3 83.8 all-gather.2
where the time goes:
time: 581 us
  waiting for transfers between devices  287 us (49%)
  blocking collectives  227 us (39%)
  matrix products  41 us (7%)
  between operations  15.6 us (3%)
  other arithmetic  6.99 us (1%)
    unnamed x3, waiting for transfers between devices  287 us
    pmax x1, blocking collectives, per_device(): whole_max = lax.pmax(part_max, ('tok', 'cen'))  96.1 us
    psum x1, blocking collectives, per_device(): lax.psum(part_sum * jnp.exp(part_max - whole_max), ('tok', 'cen'))  94.9 us
    all_gather x1, blocking collectives, per_device(): lax.all_gather(nearest, 'tok', axis=0, tiled=True)  36.5 us
    dot_general x16, matrix products, local_scores(): lax.dot_general(tblock, centroids, (((1,), (1,)), ((), ())), preferred_el...  23.7 us
    dot_general x8, matrix products, second_pass(): lax.dot_general(weight, tblock, (((0,), (0,)), ((), ())), preferred_eleme...  12.1 us
  transfers between devices with their start and end apart: 2, of which 1 were waited for; matrix products, arithmetic and copies ran while one was open for 0% of the time, Pallas kernels for 0%

commit v1 on v0

v1 whole, which is shorter than its diff:
```python
import functools
import math

import jax
import jax.numpy as jnp
from jax import lax
from jax.experimental import pallas as pl
from jax.experimental.pallas import tpu as pltpu
from jax.sharding import PartitionSpec as P

MESH = pl.DeviceIdType.MESH
NX, NY, NZ = 4, 8, 8
N_TOK, N_CEN = 32, 16
ROWS = 128
WIDTH = 128
LOCAL = 1024
CHUNK = 256
LN2 = math.log(2.0)


def ring(s):
    half = (s + 1) // 2
    return half * (2 * (s % 2) - 1)


def loop(lo, hi, body):
    def step(i, carry):
        body(i)
        return carry

    lax.fori_loop(lo, hi, step, 0)


def split3(v):
    hi = v.astype(jnp.bfloat16).astype(jnp.float32)
    mid = (v - hi).astype(jnp.bfloat16).astype(jnp.float32)
    return hi, mid, v - hi - mid


def kernel(
    tok_ref, ids_ref, cen_ref, lp_ref, upd_ref, norm_ref, res_ref,
    tok_all, ids_all, cen2, cen_aug, e_ref, g_ref, m_ref, l_send, l_cen, l_tok, l_all, flat,
    cols, py, pr, r_send, r_recv, tok_f32,
    tok_s, tok_r, fwd_s, fwd_r, ids_s, ids_r, cen_s, cen_r,
    lc_s, lc_r, lt_s, lt_r, la_s, la_r, py_s, py_r, rt_s, rt_r,
):
    t = lax.axis_index("tok")
    n = lax.axis_index("cen")
    x, z = t % NX, t // NX
    y, c = n // 2, n % 2
    sib = (t, y * 2 + 1 - c)
    unit = math.log2(math.e) / math.sqrt(WIDTH)

    def copy(src, dst, send, recv, dev):
        return pltpu.make_async_remote_copy(
            src_ref=src, dst_ref=dst, send_sem=send, recv_sem=recv, device_id=dev, device_id_type=MESH
        )

    barrier = pltpu.get_barrier_semaphore()

    def greet_tok(r):
        pl.semaphore_signal(barrier, inc=1, device_id=((t + r) % N_TOK, n), device_id_type=MESH)

    def greet_cen(r):
        pl.semaphore_signal(barrier, inc=1, device_id=(t, (n + r) % N_CEN), device_id_type=MESH)

    loop(1, N_TOK, greet_tok)
    loop(1, N_CEN, greet_cen)

    tok_all[pl.ds(t, 1)] = tok_ref[...][None]
    tok_f32[...] = tok_ref[...].astype(jnp.float32)
    ids_all[pl.ds(t, 1)] = ids_ref[...][None]
    cen2[pl.ds(c, 1)] = cen_ref[...][None]
    lane = lax.broadcasted_iota(jnp.int32, (ROWS, WIDTH), 1)
    lp_cols = jnp.transpose(lp_ref[...] * math.sqrt(WIDTH))
    for a in range(LOCAL // ROWS):
        hi, mid, low = split3(lp_cols[:, a : a + 1])
        extra = jnp.where(lane == 0, hi, jnp.where(lane == 1, mid, jnp.where(lane == 2, low, 0.0)))
        cen_aug[a * ROWS : (a + 1) * ROWS, WIDTH:] = extra.astype(jnp.bfloat16)
    cen_aug[:, :WIDTH] = cen_ref[...]

    pl.semaphore_wait(barrier, N_TOK - 1 + N_CEN - 1)

    def ids_copy(r):
        return copy(ids_ref, ids_all.at[t], ids_s.at[r], ids_r.at[r], ((t + r) % N_TOK, n))

    def cen_copy():
        return copy(cen_ref, cen2.at[c], cen_s, cen_r, sib)

    def tok_copy(s, q):
        xr = (c + s) % 2 + 2 * q
        dev = (((z - ring(s) + NZ) % NZ) * NX + (x - xr + NX) % NX, n)
        return copy(tok_ref, tok_all.at[t], tok_s.at[s, q], tok_r.at[s, q], dev)

    def fwd_copy(s, q):
        xr = (c + s) % 2 + 2 * q
        block = ((z + ring(s) + NZ) % NZ) * NX + (x + xr) % NX
        return copy(tok_all.at[block], tok_all.at[block], fwd_s.at[s, q], fwd_r.at[s, q], sib)

    def mine(s, q, core):
        return (s * 4 + q * 2 + (core + s) % 2) > 0

    loop(1, N_TOK, lambda r: ids_copy(r).start())
    cen_copy().start()

    def send_tokens(s):
        for q in range(2):
            @pl.when(mine(s, q, c))
            def _():
                tok_copy(s, q).start()

    loop(0, NZ, send_tokens)

    def receive(s):
        for q in range(2):
            @pl.when(mine(s, q, c))
            def _():
                tok_copy(s, q).wait_recv()
                fwd_copy(s, q).start()

    ones = jnp.where(lax.broadcasted_iota(jnp.int32, (CHUNK, WIDTH), 1) < 3, 1.0, 0.0).astype(jnp.bfloat16)

    def lc_copy(ch):
        return copy(l_send.at[ch], l_cen.at[n], lc_s.at[ch], lc_r.at[n], (t, ch))

    def score(s):
        for q in range(2):
            @pl.when(mine(s, q, 1 - c))
            def _():
                fwd_copy(s, q).wait_recv()
        zz = (z + ring(s) + NZ) % NZ

        def chunk(h):
            ch = 2 * zz + h
            tk = tok_all[pl.ds(2 * ch, 2)].reshape(CHUNK, WIDTH)
            raw = lax.dot_general(
                cen_aug[...], jnp.concatenate([tk, ones], axis=1),
                (((1,), (1,)), ((), ())), preferred_element_type=jnp.float32,
            )
            top = jnp.max(raw, axis=0, keepdims=True)
            e = jnp.exp2((raw - top) * unit)
            e_ref[:, pl.ds(pl.multiple_of(ch * CHUNK, CHUNK), CHUNK)] = e.astype(jnp.bfloat16)
            total = jnp.sum(e, axis=0, keepdims=True)
            m_ref[pl.ds(ch, 1)] = (top * unit)[None]
            part = top * unit + jnp.log2(total)
            l_send[pl.ds(ch, 1)] = part[None]

            @pl.when(ch != n)
            def _():
                lc_copy(ch).start()

            @pl.when(ch == n)
            def _():
                l_cen[pl.ds(ch, 1)] = part[None]

        loop(0, 2, chunk)

    def py_copy(r):
        to = (y + r) % NY
        return copy(py.at[to], pr.at[r], py_s.at[r], py_r.at[r], (t, to * 2 + c))

    def pick():
        loop(1, N_TOK, lambda r: ids_copy(r).wait_recv())
        cen_copy().wait_recv()
        first = (t * N_CEN + y * 2) * LOCAL
        rel = (ids_all[...].reshape(N_TOK, ROWS) - first).astype(jnp.float32)
        rel = jnp.transpose(rel).reshape(NY, 2, 8, N_TOK)
        rel = jnp.where(c == 0, rel[:, 0], rel[:, 1]).reshape(NY * 8, N_TOK)
        for p in range(N_TOK // 2):
            one = jnp.broadcast_to(rel[:, 2 * p : 2 * p + 1], (NY * 8, WIDTH)).reshape(NY, 1, 8, WIDTH)
            two = jnp.broadcast_to(rel[:, 2 * p + 1 : 2 * p + 2], (NY * 8, WIDTH)).reshape(NY, 1, 8, WIDTH)
            cols[p] = jnp.concatenate([one, two], axis=1).reshape(ROWS, WIDTH)
        at = lax.broadcasted_iota(jnp.int32, (1, WIDTH), 1).astype(jnp.float32)

        def part(g):
            want = cols[pl.ds(4 * g, 4)].reshape(4 * ROWS, WIDTH)
            hot = jnp.concatenate(
                [jnp.where(want == at + float(WIDTH * b), 1.0, 0.0).astype(jnp.bfloat16) for b in range(2 * LOCAL // WIDTH)],
                axis=1,
            )
            got = jnp.dot(hot, cen2[...].reshape(2 * LOCAL, WIDTH), preferred_element_type=jnp.float32)
            got = got.astype(jnp.bfloat16).reshape(4, NY, 16, WIDTH)
            for k in range(4):
                py[:, pl.ds(pl.multiple_of((4 * g + k) * 16, 16), 16), :] = got[k]

        loop(0, 4, part)
        loop(1, NY, lambda r: py_copy(r).start())

    def step(s):
        @pl.when(s < NZ)
        def _():
            receive(s)

        @pl.when(s > 0)
        def _():
            score(s - 1)

        @pl.when(s == 4)
        def _():
            pick()

    loop(0, NZ + 1, step)

    def lse(v):
        top = jnp.max(v, axis=0)
        return top + jnp.log2(jnp.sum(jnp.exp2(v - top[None]), axis=0))

    def lc_wait(r):
        src = (n + r) % N_CEN
        copy(l_send.at[src], l_cen.at[src], lc_s.at[src], lc_r.at[src], (t, src)).wait_recv()

    def lt_copy(r):
        return copy(l_tok.at[t], l_tok.at[t], lt_s.at[r], lt_r.at[r], ((t + r) % N_TOK, n))

    def la_copy(r):
        return copy(l_all.at[n], l_all.at[n], la_s.at[r], la_r.at[r], (t, (n + r) % N_CEN))

    loop(1, N_CEN, lc_wait)
    l_tok[pl.ds(t, 1)] = lse(l_cen[...])[None]
    loop(1, N_TOK, lambda r: lt_copy(r).start())

    def rt_copy(r):
        to = (t + r) % N_TOK
        return copy(r_send.at[to], r_recv.at[t], rt_s.at[r], rt_r.at[r], (to, n))

    loop(1, NY, lambda r: py_copy(r).wait_recv())
    rows = py[pl.ds(y, 1)][0].astype(jnp.float32)
    for r in range(1, NY):
        rows = rows + pr[r].astype(jnp.float32)
    r_send[...] = rows.reshape(N_TOK, 8, WIDTH)
    loop(1, N_TOK, lambda r: rt_copy(r).start())
    r_recv[pl.ds(t, 1)] = r_send[pl.ds(t, 1)]

    loop(1, N_TOK, lambda r: lt_copy(r).wait_recv())
    l_all[pl.ds(n, 1)] = lse(l_tok[...])[None]
    loop(1, N_CEN, lambda r: la_copy(r).start())
    loop(1, N_CEN, lambda r: la_copy(r).wait_recv())

    for ch in range(N_CEN):
        g = jnp.exp2(m_ref[ch] - l_all[ch])
        flat[2 * ch : 2 * ch + 1, :] = g[:, :ROWS]
        flat[2 * ch + 1 : 2 * ch + 2, :] = g[:, ROWS:]
    g_cols = jnp.transpose(flat[...])
    for i in range(N_TOK):
        g = jnp.broadcast_to(g_cols[:, i : i + 1], (ROWS, WIDTH))
        g_hi = g.astype(jnp.bfloat16).astype(jnp.float32)
        g_ref[i * ROWS : (i + 1) * ROWS, :WIDTH] = (tok_all[i].astype(jnp.float32) * g).astype(jnp.bfloat16)
        g_ref[i * ROWS : (i + 1) * ROWS, WIDTH:] = jnp.where(lane < 64, g_hi, g - g_hi).astype(jnp.bfloat16)

    def final(j):
        at = pl.ds(pl.multiple_of(j * 256, 256), 256)
        out = jnp.dot(e_ref[at, :], g_ref[...], preferred_element_type=jnp.float32)
        mass = out[:, WIDTH : WIDTH + 1] + out[:, WIDTH + 64 : WIDTH + 65]
        upd_ref[at, :] = (out[:, :WIDTH] / mass).astype(jnp.bfloat16)

    loop(0, LOCAL // 256, final)

    own = l_all[pl.ds(t // 2, 1)][0] * LN2
    norm_ref[...] = jnp.where(t % 2 == 0, own[:, :ROWS], own[:, ROWS:])

    loop(1, N_TOK, lambda r: rt_copy(r).wait_recv())
    picked = jnp.sum(r_recv[...], axis=0)
    res_ref[...] = tok_f32[pl.ds(pl.multiple_of(n * 8, 8), 8), :] - picked

    def sent_tokens(s):
        for q in range(2):
            @pl.when(mine(s, q, c))
            def _():
                tok_copy(s, q).wait_send()
                fwd_copy(s, q).wait_send()

    loop(0, NZ, sent_tokens)
    cen_copy().wait_send()

    def sent_tok(r):
        ids_copy(r).wait_send()
        lt_copy(r).wait_send()
        rt_copy(r).wait_send()

    def sent_cen(r):
        lc_copy((n + r) % N_CEN).wait_send()
        la_copy(r).wait_send()

    loop(1, N_TOK, sent_tok)
    loop(1, N_CEN, sent_cen)
    loop(1, NY, lambda r: py_copy(r).wait_send())


def per_device(tokens, nearest, centroids, log_prior):
    bf, f32, dma = jnp.bfloat16, jnp.float32, pltpu.SemaphoreType.DMA
    upd, norm, res = pl.pallas_call(
        kernel,
        out_shape=(
            jax.ShapeDtypeStruct((LOCAL, WIDTH), bf),
            jax.ShapeDtypeStruct((1, ROWS), f32),
            jax.ShapeDtypeStruct((8, WIDTH), f32),
        ),
        in_specs=[pl.BlockSpec(memory_space=pltpu.VMEM)] * 4,
        out_specs=(pl.BlockSpec(memory_space=pltpu.VMEM),) * 3,
        scratch_shapes=[
            pltpu.VMEM((N_TOK, ROWS, WIDTH), bf),
            pltpu.VMEM((N_TOK, 1, ROWS), jnp.int32),
            pltpu.VMEM((2, LOCAL, WIDTH), bf),
            pltpu.VMEM((LOCAL, 2 * WIDTH), bf),
            pltpu.VMEM((LOCAL, N_TOK * ROWS), bf),
            pltpu.VMEM((N_TOK * ROWS, 2 * WIDTH), bf),
            pltpu.VMEM((N_CEN, 1, CHUNK), f32),
            pltpu.VMEM((N_CEN, 1, CHUNK), f32),
            pltpu.VMEM((N_CEN, 1, CHUNK), f32),
            pltpu.VMEM((N_TOK, 1, CHUNK), f32),
            pltpu.VMEM((N_CEN, 1, CHUNK), f32),
            pltpu.VMEM((N_TOK, ROWS), f32),
            pltpu.VMEM((N_TOK // 2, ROWS, WIDTH), f32),
            pltpu.VMEM((NY, N_TOK * 8, WIDTH), bf),
            pltpu.VMEM((NY, N_TOK * 8, WIDTH), bf),
            pltpu.VMEM((N_TOK, 8, WIDTH), f32),
            pltpu.VMEM((N_TOK, 8, WIDTH), f32),
            pltpu.VMEM((ROWS, WIDTH), f32),
            dma((NZ, 2)), dma((NZ, 2)), dma((NZ, 2)), dma((NZ, 2)),
            dma((N_TOK,)), dma((N_TOK,)), dma, dma,
            dma((N_CEN,)), dma((N_CEN,)), dma((N_TOK,)), dma((N_TOK,)),
            dma((N_CEN,)), dma((N_CEN,)), dma((NY,)), dma((NY,)),
            dma((N_TOK,)), dma((N_TOK,)),
        ],
        compiler_params=pltpu.CompilerParams(
            collective_id=0, has_side_effects=True, vmem_limit_bytes=48 << 20
        ),
    )(tokens, nearest.reshape(1, ROWS), centroids, log_prior.reshape(LOCAL // ROWS, ROWS))
    return upd, norm.reshape(ROWS), res.astype(bf)


def solution(mesh):
    return jax.shard_map(
        per_device,
        mesh=mesh,
        in_specs=(P("tok", None), P("tok"), P(("tok", "cen"), None), P(("tok", "cen"))),
        out_specs=(P(("tok", "cen"), None), P("tok"), P(("tok", "cen"), None)),
        check_vma=False,
    )
```

time: 581 us -> 71.2 us (0.12)
  waiting for transfers between devices: 287 us -> 0 us
  blocking collectives: 227 us -> 0 us
  Pallas kernels: 0 us -> 65.5 us
  matrix products: 41 us -> 0 us
  between operations: 15.6 us -> 0.65 us
  other arithmetic: 6.99 us -> 0.58 us
    unnamed x3 -> x0, waiting for transfers between devices: 287 us -> none
    pmax x1 -> x0, blocking collectives: 96.1 us -> none  [per_device(): whole_max = lax.pmax(part_max, ('tok', 'cen'))]
    psum x1 -> x0, blocking collectives: 94.9 us -> none  [per_device(): lax.psum(part_sum * jnp.exp(part_max - whole_max), ('tok', 'cen'))]
    pallas_call x0 -> x1, Pallas kernels: none -> 65.5 us  [per_device(): pl.pallas_call(kernel, out_shape=(jax.ShapeDtypeStruct((LOCAL, WIDTH), bf...]
    dot_general x25 -> x0, matrix products: 41 us -> none  [the longest x16 23.7 us: local_scores(): lax.dot_general(tblock, centroids, (((1,), (1,)), ((), ())), preferred_el...]
    all_gather x1 -> x0, blocking collectives: 36.5 us -> none  [per_device(): lax.all_gather(nearest, 'tok', axis=0, tiled=True)]
  transfers between devices with their start and end apart: 2 -> 0, of which waited for: 1 -> 0; matrix products, arithmetic and copies ran while one was open for 0% -> 0% of each run, Pallas kernels for 0% -> 0%
where the time goes in v1:
time: 71.2 us; the launch traced here: 71 us
  Pallas kernels  65.5 us (92%)
  local copies, waits for them, and re-layouts  4.25 us (6%)
    pallas_call x1, Pallas kernels, per_device(): pl.pallas_call(kernel, out_shape=(jax.ShapeDtypeStruct((LOCAL, WIDTH), bf...  65.5 us
    unnamed x10, local copies, waits for them, and re-layouts  4.25 us

profile of v1, /device:TPU:1, one launch (start us, length us, event | category | flops | bytes accessed | tf_op | source)
XLA Modules:
  0.0 71.0 jit_solution(10362784923015291643)
XLA Ops:
  0.6 0.0 copy-start.3
  0.6 0.6 copy-done.3
  1.3 0.0 copy-start
  1.3 0.9 %copy-done = bf16[1024,128]{1,0:T(8,128)(2,1)S(1)} copy-done((bf16[1024,128]{1,0:T(8,128)(2,1)S(1)}, bf16[1024,128]{1,0:T(8,128)(2,1)}, u32[]{:S(2)}) %copy-start) | copy-done | bytes 262168
  2.2 0.0 copy-start.1
  2.2 0.8 %copy-done.1 = bf16[128,128]{1,0:T(8,128)(2,1)S(1)} copy-done((bf16[128,128]{1,0:T(8,128)(2,1)S(1)}, bf16[128,128]{1,0:T(8,128)(2,1)}, u32[]{:S(2)}) %copy-start.1) | copy-done | bytes 32792
  3.0 0.0 copy-start.2
  3.0 0.7 copy-done.2
  3.7 65.5 %shard_map.67 = (bf16[1024,128]{1,0:T(8,128)(2,1)S(1)}, f32[1,128]{1,0:T(1,128)S(1)}, f32[8,128]{1,0:T(8,128)S(1)}) custom-call(bf16[128,128]{1,0:T(8,128)(2,1)S(1)} %copy-done.1, s32[1,128]{1,0:T(1,128)S(1)} %bitcast.4, bf16[1024,128]{1,0:T(8,128)(2,1)S(1)} %copy-done, f32[8,128]{1,0:T(8,128)S(1)} %bitcast.3), custom_call_target="tpu_custom_call" | custom-call | tf_op jit(solution)/shard_map/pallas_call | solution.py:291
  69.2 0.6 convert_element_type.3
  69.8 0.7 copy.9
  70.5 0.5 copy.10
Async XLA Ops:
  0.6 0.7 copy-start.3
  1.3 0.9 %copy-start = (bf16[1024,128]{1,0:T(8,128)(2,1)S(1)}, bf16[1024,128]{1,0:T(8,128)(2,1)}, u32[]{:S(2)}) copy-start(bf16[1024,128]{1,0:T(8,128)(2,1)} %cen_ref.1) | copy-start | bytes 786436
  2.2 0.8 %copy-start.1 = (bf16[128,128]{1,0:T(8,128)(2,1)S(1)}, bf16[128,128]{1,0:T(8,128)(2,1)}, u32[]{:S(2)}) copy-start(bf16[128,128]{1,0:T(8,128)(2,1)} %tok_ref.1) | copy-start | bytes 98308
  3.0 0.7 copy-start.2

commit v2 on v1

v2 whole, which is shorter than its diff:
```python
import functools
import math

import jax
import jax.numpy as jnp
from jax import lax
from jax.experimental import pallas as pl
from jax.experimental.pallas import tpu as pltpu
from jax.sharding import PartitionSpec as P

MESH = pl.DeviceIdType.MESH
NX, NY, NZ = 4, 8, 8
N_TOK, N_CEN = 32, 16
ROWS = 128
WIDTH = 128
LOCAL = 1024
CHUNK = 256
LN2 = math.log(2.0)
VMEM_LIMIT = 60 << 20


def ring(s):
    half = (s + 1) // 2
    return half * (2 * (s % 2) - 1)


def loop(lo, hi, body):
    def step(i, carry):
        body(i)
        return carry

    lax.fori_loop(lo, hi, step, 0)


def split3(v):
    hi = v.astype(jnp.bfloat16).astype(jnp.float32)
    mid = (v - hi).astype(jnp.bfloat16).astype(jnp.float32)
    return hi, mid, v - hi - mid


def kernel(
    tok_hbm, ids_hbm, cen_hbm, lp_hbm, upd_ref, norm_ref, res_ref,
    tok_all, ids_all, cen2, lp_ref, cen_aug, e_ref, acc, m_ref, l_send, l_cen, l_tok, l_all,
    cols, ya_out, ya_in, ta_out, ta_in, xb_out, xb_in, yb_out, yb_in, zb_out, zb_in, tok_f32,
    in_s, z_s, z_r, x_s, x_r, f_s, f_r, idz_s, idz_r, idx_s, idx_r, cen_s, cen_r,
    lc_s, lc_r, lt_s, lt_r, la_s, la_r, ya_s, ya_r, ta_s, ta_r, xb_s, xb_r, yb_s, yb_r, zb_s, zb_r,
):
    t = lax.axis_index("tok")
    n = lax.axis_index("cen")
    x, z = t % NX, t // NX
    y, c = n // 2, n % 2
    sib = (t, y * 2 + 1 - c)
    unit = math.log2(math.e) / math.sqrt(WIDTH)

    def at_x(k):
        return (z * NX + (x + k) % NX, n)

    def at_y(k):
        return (t, ((y + k) % NY) * 2 + c)

    def at_z(k):
        return (((z + k) % NZ) * NX + x, n)

    def copy(src, dst, send, recv, dev):
        return pltpu.make_async_remote_copy(
            src_ref=src, dst_ref=dst, send_sem=send, recv_sem=recv, device_id=dev, device_id_type=MESH
        )

    barrier = pltpu.get_barrier_semaphore()

    def greet(dev):
        pl.semaphore_signal(barrier, inc=1, device_id=dev, device_id_type=MESH)

    loop(1, NZ, lambda k: greet(at_z(k)))
    loop(1, NY, lambda k: greet(at_y(k)))
    loop(1, NX, lambda k: greet(at_x(k)))
    greet(sib)

    fetch = [
        pltpu.make_async_copy(tok_hbm, tok_all.at[t], in_s.at[0]),
        pltpu.make_async_copy(ids_hbm, ids_all.at[x * NZ + z], in_s.at[1]),
        pltpu.make_async_copy(cen_hbm, cen2.at[c], in_s.at[2]),
        pltpu.make_async_copy(lp_hbm, lp_ref, in_s.at[3]),
    ]
    for f in fetch:
        f.start()
    for f in fetch:
        f.wait()
    tok_f32[...] = tok_all[pl.ds(t, 1)][0].astype(jnp.float32)
    lane = lax.broadcasted_iota(jnp.int32, (ROWS, WIDTH), 1)
    lp_cols = jnp.transpose(lp_ref[...] * math.sqrt(WIDTH))
    for a in range(LOCAL // ROWS):
        hi, mid, low = split3(lp_cols[:, a : a + 1])
        extra = jnp.where(lane == 0, hi, jnp.where(lane == 1, mid, jnp.where(lane == 2, low, 0.0)))
        cen_aug[a * ROWS : (a + 1) * ROWS, WIDTH:] = extra.astype(jnp.bfloat16)
    cen_aug[:, :WIDTH] = cen2[pl.ds(c, 1)][0]

    pl.semaphore_wait(barrier, NZ - 1 + NY - 1 + NX - 1 + 1)

    def idz_copy(k):
        return copy(ids_all.at[x * NZ + z], ids_all.at[x * NZ + z], idz_s.at[k], idz_r.at[k], at_z(k))

    def idx_copy(k):
        rows = pl.ds(x * NZ, NZ)
        return copy(ids_all.at[rows], ids_all.at[rows], idx_s.at[k], idx_r.at[k], at_x(k))

    def cen_copy():
        return copy(cen2.at[c], cen2.at[c], cen_s, cen_r, sib)

    def z_copy(s):
        return copy(tok_all.at[t], tok_all.at[t], z_s.at[s], z_r.at[s], at_z(NZ - ring(s)))

    def block(s, k):
        return ((z + ring(s) + NZ) % NZ) * NX + (x + k) % NX

    def x_copy(s, k):
        b = block(s, 0)
        return copy(tok_all.at[b], tok_all.at[b], x_s.at[s, k], x_r.at[s, k], at_x(NX - k))

    def f_copy(s, k):
        b = block(s, k)
        return copy(tok_all.at[b], tok_all.at[b], f_s.at[s, k], f_r.at[s, k], sib)

    def if_mine(s, core, todo):
        pl.when(s % 2 == core)(todo)

    loop(1, NZ, lambda k: idz_copy(k).start())
    loop(1, NZ, lambda s: if_mine(s, c, lambda: z_copy(s).start()))
    cen_copy().start()

    def receive_z(s):
        def todo():
            @pl.when(s > 0)
            def _():
                z_copy(s).wait_recv()

            for k in range(1, NX):
                x_copy(s, k).start()

            @pl.when(s > 0)
            def _():
                f_copy(s, 0).start()

        if_mine(s, c, todo)

    def receive_x(s):
        def todo():
            for k in range(1, NX):
                x_copy(s, k).wait_recv()
                f_copy(s, k).start()

        if_mine(s, c, todo)

    ones = jnp.where(lax.broadcasted_iota(jnp.int32, (CHUNK, WIDTH), 1) < 3, 1.0, 0.0).astype(jnp.bfloat16)

    def lc_copy(ch):
        return copy(l_send.at[ch], l_cen.at[n], lc_s.at[ch], lc_r.at[n], (t, ch))

    def score(s):
        def todo():
            @pl.when(s > 0)
            def _():
                f_copy(s, 0).wait_recv()

            for k in range(1, NX):
                f_copy(s, k).wait_recv()

        if_mine(s, 1 - c, todo)
        zz = (z + ring(s) + NZ) % NZ
        parts = []
        for h in range(2):
            ch = 2 * zz + h
            tk = tok_all[pl.ds(2 * ch, 2)].reshape(CHUNK, WIDTH)
            raw = lax.dot_general(
                cen_aug[...], jnp.concatenate([tk, ones], axis=1),
                (((1,), (1,)), ((), ())), preferred_element_type=jnp.float32,
            )
            top = jnp.max(raw, axis=0, keepdims=True)
            e = jnp.exp2((raw - top) * unit)
            e_ref[:, pl.ds(pl.multiple_of(ch * CHUNK, CHUNK), CHUNK)] = e.astype(jnp.bfloat16)
            total = jnp.sum(e, axis=0, keepdims=True)
            m_ref[pl.ds(ch, 1)] = (top * unit)[None]
            part = top * unit + jnp.log2(total)
            l_send[pl.ds(ch, 1)] = part[None]
            parts.append(part)
        for h in range(2):
            ch = 2 * zz + h
            part = parts[h]

            @pl.when(ch != n)
            def _():
                lc_copy(ch).start()

            @pl.when(ch == n)
            def _():
                l_cen[pl.ds(ch, 1)] = part[None]

    def ya_copy(k):
        return copy(ya_out.at[(y + k) % NY], ya_in.at[k], ya_s.at[k], ya_r.at[k], at_y(k))

    def xb_copy(k):
        return copy(xb_out.at[(x + k) % NX], xb_in.at[k], xb_s.at[k], xb_r.at[k], at_x(k))

    def yb_copy(k):
        return copy(yb_out.at[(y + k) % NY], yb_in.at[k], yb_s.at[k], yb_r.at[k], at_y(k))

    def pick():
        loop(1, NX, lambda k: idx_copy(k).wait_recv())
        first = (t * N_CEN + y * 2) * LOCAL
        rel = (ids_all[...].reshape(N_TOK, ROWS) - first).astype(jnp.float32)
        rel = jnp.transpose(rel).reshape(NY, 2, 8, N_TOK)
        rel = jnp.where(c == 0, rel[:, 0], rel[:, 1]).reshape(NY * 8, N_TOK)

        def spread(zb, xb):
            i = xb * NZ + zb
            return jnp.broadcast_to(rel[:, i : i + 1], (NY * 8, WIDTH)).reshape(NY, 1, 8, WIDTH)

        for p in range(N_TOK // 2):
            if p < 8:
                one, two = (p // 2, (2 * p) % NX), (p // 2, (2 * p) % NX + 1)
            else:
                one, two = (2 * (p // 4), p % NX), (2 * (p // 4) + 1, p % NX)
            cols[p] = jnp.concatenate([spread(*one), spread(*two)], axis=1).reshape(ROWS, WIDTH)
        at = lax.broadcasted_iota(jnp.int32, (1, WIDTH), 1).astype(jnp.float32)

        def part(g):
            want = cols[pl.ds(4 * g, 4)].reshape(4 * ROWS, WIDTH)
            hot = jnp.concatenate(
                [jnp.where(want == at + float(WIDTH * b), 1.0, 0.0).astype(jnp.bfloat16) for b in range(2 * LOCAL // WIDTH)],
                axis=1,
            )
            got = jnp.dot(hot, cen2[...].reshape(2 * LOCAL, WIDTH), preferred_element_type=jnp.float32)
            return got.astype(jnp.bfloat16).reshape(4, NY, 16, WIDTH)

        def part_a(g):
            got = part(g)
            for k in range(4):
                ya_out[:, pl.ds(pl.multiple_of((4 * g + k) * 16, 16), 16), :] = got[k]

        def part_b(g):
            got = part(g)
            for k in range(4):
                xb_out[k, :, pl.ds(pl.multiple_of((g - 2) * 16, 16), 16), :] = got[k]

        loop(0, 2, part_a)
        loop(1, NY, lambda k: ya_copy(k).start())
        loop(2, 4, part_b)
        loop(1, NX, lambda k: xb_copy(k).start())

    def ids_along_x():
        loop(1, NZ, lambda k: idz_copy(k).wait_recv())
        loop(1, NX, lambda k: idx_copy(k).start())

    receive_z(0)
    cen_copy().wait_recv()
    loop(1, 3, receive_z)
    receive_x(0)
    loop(3, 5, receive_z)
    ids_along_x()

    def step(s):
        @pl.when(s == 1)
        def _():
            loop(5, NZ, receive_z)
            loop(1, 3, receive_x)

        @pl.when((s >= 1) & (s + 2 < NZ))
        def _():
            receive_x(s + 2)

        score(s)

    loop(0, NZ, step)
    pick()

    def tok_of(j):
        return ((z + ring(7 - j // NX) + NZ) % NZ) * NX + (x + 1 + j % NX) % NX

    def cen_of(j):
        return ((y + ring(7 - j // 2) + NY) % NY) * 2 + (c + 1 + j) % 2

    def lse(v):
        top = jnp.max(v, axis=0)
        return top + jnp.log2(jnp.sum(jnp.exp2(v - top[None]), axis=0))

    def lc_wait(j):
        src = cen_of(j)
        copy(l_send.at[src], l_cen.at[src], lc_s.at[src], lc_r.at[src], (t, src)).wait_recv()

    def lt_copy(to):
        return copy(l_tok.at[t], l_tok.at[t], lt_s.at[to], lt_r.at[t], (to, n))

    def lt_wait(j):
        src = tok_of(j)
        copy(l_tok.at[src], l_tok.at[src], lt_s.at[src], lt_r.at[src], (src, n)).wait_recv()

    def la_copy(to):
        return copy(l_all.at[n], l_all.at[n], la_s.at[to], la_r.at[n], (t, to))

    def la_wait(src):
        copy(l_all.at[src], l_all.at[src], la_s.at[src], la_r.at[src], (t, src)).wait_recv()

    def ta_copy(to):
        return copy(ta_out.at[to], ta_in.at[t], ta_s.at[to], ta_r.at[t], (to, n))

    def ta_wait(src):
        copy(ta_out.at[0], ta_in.at[src], ta_s.at[0], ta_r.at[src], (src, n)).wait_recv()

    half = NZ // 2

    def zb_copy(zt):
        dev = (zt * NX + x, n)
        return copy(zb_out.at[zt - half], zb_in.at[z], zb_s.at[zt], zb_r.at[z], dev)

    def zb_wait(src):
        copy(zb_out.at[0], zb_in.at[src], zb_s.at[0], zb_r.at[src], (src * NX + x, n)).wait_recv()

    loop(1, NX, lambda k: xb_copy(k).wait_recv())
    rows = xb_out[pl.ds(x, 1)][0].astype(jnp.float32)
    for k in range(1, NX):
        rows = rows + xb_in[k].astype(jnp.float32)
    yb_out[...] = rows.astype(jnp.bfloat16)
    loop(1, NY, lambda k: yb_copy(k).start())

    loop(0, N_CEN - 1, lc_wait)
    l_tok[pl.ds(t, 1)] = lse(l_cen[...])[None]
    loop(0, N_TOK - 1, lambda j: lt_copy(tok_of(j)).start())

    loop(1, NY, lambda k: ya_copy(k).wait_recv())
    rows = ya_out[pl.ds(y, 1)][0].astype(jnp.float32)
    for k in range(1, NY):
        rows = rows + ya_in[k].astype(jnp.float32)
    ta_out[...] = rows.reshape(half * NX, 8, WIDTH)

    def ta_each(act):
        def body(to):
            @pl.when(to != t)
            def _():
                act(to)

        loop(0, half * NX, body)

    ta_each(lambda to: ta_copy(to).start())

    loop(1, NY, lambda k: yb_copy(k).wait_recv())
    rows = yb_out[pl.ds(y, 1)][0].astype(jnp.float32)
    for k in range(1, NY):
        rows = rows + yb_in[k].astype(jnp.float32)
    zb_out[...] = rows.reshape(half, 8, WIDTH)

    def zb_each(act):
        def body(zt):
            @pl.when(zt != z)
            def _():
                act(zt)

        loop(half, NZ, body)

    zb_each(lambda zt: zb_copy(zt).start())

    loop(0, N_TOK - 1, lt_wait)
    l_all[pl.ds(n, 1)] = lse(l_tok[...])[None]
    loop(0, N_CEN - 1, lambda j: la_copy(cen_of(j)).start())

    def product(k):
        yy = (y + ring(k) + NY) % NY
        rows = []
        for h in range(2):
            ch = 2 * yy + h
            g_row = jnp.exp2(m_ref[pl.ds(ch, 1)][0] - l_all[pl.ds(ch, 1)][0])
            for b in range(2):
                g = jnp.transpose(jnp.broadcast_to(g_row[:, b * ROWS : (b + 1) * ROWS], (WIDTH, ROWS)))
                g_hi = g.astype(jnp.bfloat16).astype(jnp.float32)
                tk = tok_all[pl.ds(2 * ch + b, 1)][0].astype(jnp.float32)
                rows.append(
                    jnp.concatenate([tk * g, jnp.where(lane < 64, g_hi, g - g_hi)], axis=1).astype(jnp.bfloat16)
                )
        e = e_ref[:, pl.ds(pl.multiple_of(yy * 2 * CHUNK, 2 * CHUNK), 2 * CHUNK)]
        return jnp.dot(e, jnp.concatenate(rows, axis=0), preferred_element_type=jnp.float32)

    for group in ((0,), (1, 2), (3, 4), (5, 6, 7)):
        for k in group:
            for h in range(2):
                ch = 2 * ((y + ring(k) + NY) % NY) + h

                @pl.when(ch != n)
                def _():
                    la_wait(ch)

        for k in group:
            if k == 0:
                acc[...] = product(k)
            else:
                acc[...] += product(k)
    mass = acc[:, WIDTH:]
    mass = mass + pltpu.roll(mass, 64, 1)
    upd_ref[...] = (acc[:, :WIDTH] / mass).astype(jnp.bfloat16)

    own = l_all[pl.ds(t // 2, 1)][0] * LN2
    norm_ref[...] = jnp.where(t % 2 == 0, own[:, :ROWS], own[:, ROWS:])

    mine = tok_f32[pl.ds(pl.multiple_of(n * 8, 8), 8), :]

    @pl.when(z < half)
    def _():
        ta_in[pl.ds(t, 1)] = ta_out[pl.ds(t, 1)]
        loop(0, N_TOK - 1, lambda j: ta_wait(tok_of(j)))
        res_ref[...] = (mine - jnp.sum(ta_in[...], axis=0)).astype(jnp.bfloat16)

    @pl.when(z >= half)
    def _():
        zb_in[pl.ds(z, 1)] = zb_out[pl.ds(z - half, 1)]
        loop(1, NZ, lambda k: zb_wait((z + k) % NZ))
        res_ref[...] = (mine - jnp.sum(zb_in[...], axis=0)).astype(jnp.bfloat16)

    def sent(s):
        def todo():
            @pl.when(s > 0)
            def _():
                z_copy(s).wait_send()
                f_copy(s, 0).wait_send()

            for k in range(1, NX):
                x_copy(s, k).wait_send()
                f_copy(s, k).wait_send()

        if_mine(s, c, todo)

    loop(0, NZ, sent)
    cen_copy().wait_send()

    def sent_axis(k):
        idz_copy(k).wait_send()
        ya_copy(k).wait_send()
        yb_copy(k).wait_send()

    def sent_x(k):
        idx_copy(k).wait_send()
        xb_copy(k).wait_send()

    def sent_cen(j):
        lc_copy(cen_of(j)).wait_send()
        la_copy(cen_of(j)).wait_send()

    loop(1, NZ, sent_axis)
    loop(1, NX, sent_x)
    loop(0, N_CEN - 1, sent_cen)
    loop(0, N_TOK - 1, lambda j: lt_copy(tok_of(j)).wait_send())
    ta_each(lambda to: ta_copy(to).wait_send())
    zb_each(lambda zt: zb_copy(zt).wait_send())


def hand_on(upd_in, norm_in, res_in, upd_ref, norm_ref, res_ref):
    upd_ref[...] = upd_in[...]
    norm_ref[...] = norm_in[...]
    res_ref[...] = res_in[...]


def per_device(tokens, nearest, centroids, log_prior):
    bf, f32, dma, vmem = jnp.bfloat16, jnp.float32, pltpu.SemaphoreType.DMA, pltpu.VMEM
    upd, norm, res = pl.pallas_call(
        kernel,
        out_shape=(
            jax.ShapeDtypeStruct((LOCAL, WIDTH), bf),
            jax.ShapeDtypeStruct((1, ROWS), f32),
            jax.ShapeDtypeStruct((8, WIDTH), bf),
        ),
        in_specs=[pl.BlockSpec(memory_space=pltpu.HBM)] * 4,
        out_specs=(pl.BlockSpec(memory_space=pltpu.VMEM),) * 3,
        scratch_shapes=[
            vmem((N_TOK, ROWS, WIDTH), bf),
            vmem((N_TOK, 1, ROWS), jnp.int32),
            vmem((2, LOCAL, WIDTH), bf),
            vmem((LOCAL // ROWS, ROWS), f32),
            vmem((LOCAL, 2 * WIDTH), bf),
            vmem((LOCAL, N_TOK * ROWS), bf),
            vmem((LOCAL, 2 * WIDTH), f32),
            vmem((N_CEN, 1, CHUNK), f32),
            vmem((N_CEN, 1, CHUNK), f32),
            vmem((N_CEN, 1, CHUNK), f32),
            vmem((N_TOK, 1, CHUNK), f32),
            vmem((N_CEN, 1, CHUNK), f32),
            vmem((N_TOK // 2, ROWS, WIDTH), f32),
            vmem((NY, ROWS, WIDTH), bf), vmem((NY, ROWS, WIDTH), bf),
            vmem((N_TOK // 2, 8, WIDTH), f32), vmem((N_TOK, 8, WIDTH), f32),
            vmem((NX, NY, 32, WIDTH), bf), vmem((NX, NY, 32, WIDTH), bf),
            vmem((NY, 32, WIDTH), bf), vmem((NY, 32, WIDTH), bf),
            vmem((NZ // 2, 8, WIDTH), f32), vmem((NZ, 8, WIDTH), f32),
            vmem((ROWS, WIDTH), f32),
            dma((4,)), dma((NZ,)), dma((NZ,)), dma((NZ, NX)), dma((NZ, NX)), dma((NZ, NX)), dma((NZ, NX)),
            dma((NZ,)), dma((NZ,)), dma((NX,)), dma((NX,)), dma, dma,
            dma((N_CEN,)), dma((N_CEN,)), dma((N_TOK,)), dma((N_TOK,)), dma((N_CEN,)), dma((N_CEN,)),
            dma((NY,)), dma((NY,)), dma((N_TOK,)), dma((N_TOK,)), dma((NX,)), dma((NX,)),
            dma((NY,)), dma((NY,)), dma((NZ,)), dma((NZ,)),
        ],
        compiler_params=pltpu.CompilerParams(
            collective_id=0, has_side_effects=True, vmem_limit_bytes=VMEM_LIMIT
        ),
    )(tokens, nearest.reshape(1, ROWS), centroids, log_prior.reshape(LOCAL // ROWS, ROWS))
    upd, norm, res = pl.pallas_call(
        hand_on,
        out_shape=tuple(jax.ShapeDtypeStruct(v.shape, v.dtype) for v in (upd, norm, res)),
        in_specs=[pl.BlockSpec(memory_space=pltpu.VMEM)] * 3,
        out_specs=(pl.BlockSpec(memory_space=pltpu.VMEM),) * 3,
        compiler_params=pltpu.CompilerParams(vmem_limit_bytes=VMEM_LIMIT),
    )(upd, norm, res)
    return upd, norm.reshape(ROWS), res


def solution(mesh):
    return jax.shard_map(
        per_device,
        mesh=mesh,
        in_specs=(P("tok", None), P("tok"), P(("tok", "cen"), None), P(("tok", "cen"))),
        out_specs=(P(("tok", "cen"), None), P("tok"), P(("tok", "cen"), None)),
        check_vma=False,
    )
```

time: 71.2 us -> 63.6 us (0.89)
  local copies, waits for them, and re-layouts: 4.25 us -> 0 us
  Pallas kernels: 65.5 us -> 62.8 us
    pallas_call x1, Pallas kernels: 65.5 us -> 61.2 us  [per_device(): pl.pallas_call(kernel, out_shape=(jax.ShapeDtypeStruct((LOCAL, WIDTH), bf...]
    unnamed x10 -> x0, local copies, waits for them, and re-layouts: 4.25 us -> none
    pallas_call x0 -> x1, Pallas kernels: none -> 1.68 us  [per_device(): pl.pallas_call(hand_on, out_shape=tuple((jax.ShapeDtypeStruct(v.shape, v....]
where the time goes in v2:
time: 63.6 us; the launch traced here: 63.5 us
  Pallas kernels  62.8 us (99%)
  between operations  0.64 us (1%)
    pallas_call x1, Pallas kernels, per_device(): pl.pallas_call(kernel, out_shape=(jax.ShapeDtypeStruct((LOCAL, WIDTH), bf...  61.2 us
    pallas_call x1, Pallas kernels, per_device(): pl.pallas_call(hand_on, out_shape=tuple((jax.ShapeDtypeStruct(v.shape, v....  1.68 us

profile of v2, /device:TPU:1, one launch (start us, length us, event | category | flops | bytes accessed | tf_op | source)
XLA Modules:
  0.0 63.5 jit_solution(7991329348371945194)
XLA Ops:
  0.6 61.2 %shard_map.67 = (bf16[1024,128]{1,0:T(8,128)(2,1)}, f32[1,128]{1,0:T(1,128)}, bf16[8,128]{1,0:T(8,128)(2,1)}) custom-call(bf16[128,128]{1,0:T(8,128)(2,1)} %tok_hbm.1, s32[1,128]{1,0:T(1,128)} %bitcast.4, bf16[1024,128]{1,0:T(8,128)(2,1)} %cen_hbm.1, f32[8,128]{1,0:T(8,128)} %bitcast.3), custom_call_target="tpu_custom_call" | custom-call | tf_op jit(solution)/shard_map/pallas_call | solution.py:461
  61.8 1.7 %shard_map.68 = (bf16[1024,128]{1,0:T(8,128)(2,1)}, f32[1,128]{1,0:T(1,128)}, bf16[8,128]{1,0:T(8,128)(2,1)}) custom-call(bf16[1024,128]{1,0:T(8,128)(2,1)} %get-tuple-element.9.upd_in, f32[1,128]{1,0:T(1,128)} %get-tuple-element.10.norm_in, bf16[8,128]{1,0:T(8,128)(2,1)} %get-tuple-element.11.res_in), custom_call_target="tpu_custom_call" | custom-call | tf_op jit(solution)/shard_map/pallas_call | solution.py:500

commit v3 on v2

--- a/solution.py
+++ b/solution.py
@@ -17,6 +17,7 @@
 CHUNK = 256
 LN2 = math.log(2.0)
 VMEM_LIMIT = 60 << 20
+PICK_B, PICK_A = 8, 8
 
 
 def ring(s):
@@ -40,7 +41,7 @@
 
 def kernel(
     tok_hbm, ids_hbm, cen_hbm, lp_hbm, upd_ref, norm_ref, res_ref,
-    tok_all, ids_all, cen2, lp_ref, cen_aug, e_ref, acc, m_ref, l_send, l_cen, l_tok, l_all,
+    tok_all, ids_all, cen2, lp_ref, cen_aug, tok_t, e_ref, acc, m_ref, l_send, l_cen, l_tok, l_all,
     cols, ya_out, ya_in, ta_out, ta_in, xb_out, xb_in, yb_out, yb_in, zb_out, zb_in, tok_f32,
     in_s, z_s, z_r, x_s, x_r, f_s, f_r, idz_s, idz_r, idx_s, idx_r, cen_s, cen_r,
     lc_s, lc_r, lt_s, lt_r, la_s, la_r, ya_s, ya_r, ta_s, ta_r, xb_s, xb_r, yb_s, yb_r, zb_s, zb_r,
@@ -93,7 +94,10 @@
         hi, mid, low = split3(lp_cols[:, a : a + 1])
         extra = jnp.where(lane == 0, hi, jnp.where(lane == 1, mid, jnp.where(lane == 2, low, 0.0)))
         cen_aug[a * ROWS : (a + 1) * ROWS, WIDTH:] = extra.astype(jnp.bfloat16)
-    cen_aug[:, :WIDTH] = cen2[pl.ds(c, 1)][0]
+    cen_aug[:LOCAL, :WIDTH] = cen2[pl.ds(c, 1)][0]
+    eye = lane == lax.broadcasted_iota(jnp.int32, (ROWS, WIDTH), 0)
+    cen_aug[LOCAL:, :WIDTH] = jnp.where(eye, 1.0, 0.0).astype(jnp.bfloat16)
+    cen_aug[LOCAL:, WIDTH:] = jnp.zeros((WIDTH, WIDTH), jnp.bfloat16)
 
     pl.semaphore_wait(barrier, NZ - 1 + NY - 1 + NX - 1 + 1)
 
@@ -175,6 +179,8 @@
                 cen_aug[...], jnp.concatenate([tk, ones], axis=1),
                 (((1,), (1,)), ((), ())), preferred_element_type=jnp.float32,
             )
+            tok_t[pl.ds(ch, 1)] = raw[LOCAL:].astype(jnp.bfloat16)[None]
+            raw = raw[:LOCAL]
             top = jnp.max(raw, axis=0, keepdims=True)
             e = jnp.exp2((raw - top) * unit)
             e_ref[:, pl.ds(pl.multiple_of(ch * CHUNK, CHUNK), CHUNK)] = e.astype(jnp.bfloat16)
@@ -204,7 +210,7 @@
     def yb_copy(k):
         return copy(yb_out.at[(y + k) % NY], yb_in.at[k], yb_s.at[k], yb_r.at[k], at_y(k))
 
-    def pick():
+    def pick_prepare():
         loop(1, NX, lambda k: idx_copy(k).wait_recv())
         first = (t * N_CEN + y * 2) * LOCAL
         rel = (ids_all[...].reshape(N_TOK, ROWS) - first).astype(jnp.float32)
@@ -221,29 +227,33 @@
             else:
                 one, two = (2 * (p // 4), p % NX), (2 * (p // 4) + 1, p % NX)
             cols[p] = jnp.concatenate([spread(*one), spread(*two)], axis=1).reshape(ROWS, WIDTH)
+
+    def part(g):
         at = lax.broadcasted_iota(jnp.int32, (1, WIDTH), 1).astype(jnp.float32)
-
-        def part(g):
-            want = cols[pl.ds(4 * g, 4)].reshape(4 * ROWS, WIDTH)
-            hot = jnp.concatenate(
-                [jnp.where(want == at + float(WIDTH * b), 1.0, 0.0).astype(jnp.bfloat16) for b in range(2 * LOCAL // WIDTH)],
-                axis=1,
-            )
-            got = jnp.dot(hot, cen2[...].reshape(2 * LOCAL, WIDTH), preferred_element_type=jnp.float32)
-            return got.astype(jnp.bfloat16).reshape(4, NY, 16, WIDTH)
-
-        def part_a(g):
-            got = part(g)
-            for k in range(4):
-                ya_out[:, pl.ds(pl.multiple_of((4 * g + k) * 16, 16), 16), :] = got[k]
-
-        def part_b(g):
-            got = part(g)
-            for k in range(4):
-                xb_out[k, :, pl.ds(pl.multiple_of((g - 2) * 16, 16), 16), :] = got[k]
-
+        want = cols[pl.ds(4 * g, 4)].reshape(4 * ROWS, WIDTH)
+        hot = jnp.concatenate(
+            [jnp.where(want == at + float(WIDTH * b), 1.0, 0.0).astype(jnp.bfloat16) for b in range(2 * LOCAL // WIDTH)],
+            axis=1,
+        )
+        got = jnp.dot(hot, cen2[...].reshape(2 * LOCAL, WIDTH), preferred_element_type=jnp.float32)
+        return got.astype(jnp.bfloat16).reshape(4, NY, 16, WIDTH)
+
+    def part_a(g):
+        got = part(g)
+        for k in range(4):
+            ya_out[:, pl.ds(pl.multiple_of((4 * g + k) * 16, 16), 16), :] = got[k]
+
+    def part_b(g):
+        got = part(g)
+        for k in range(4):
+            xb_out[k, :, pl.ds(pl.multiple_of((g - 2) * 16, 16), 16), :] = got[k]
+
+    def pick_a():
         loop(0, 2, part_a)
         loop(1, NY, lambda k: ya_copy(k).start())
+
+    def pick_b():
+        pick_prepare()
         loop(2, 4, part_b)
         loop(1, NX, lambda k: xb_copy(k).start())
 
@@ -268,10 +278,17 @@
         def _():
             receive_x(s + 2)
 
+        if PICK_B < NZ:
+            pl.when(s == PICK_B)(pick_b)
+        if PICK_A < NZ:
+            pl.when(s == PICK_A)(pick_a)
         score(s)
 
     loop(0, NZ, step)
-    pick()
+    if PICK_B >= NZ:
+        pick_b()
+    if PICK_A >= NZ:
+        pick_a()
 
     def tok_of(j):
         return ((z + ring(7 - j // NX) + NZ) % NZ) * NX + (x + 1 + j % NX) % NX
@@ -314,6 +331,10 @@
 
     def zb_wait(src):
         copy(zb_out.at[0], zb_in.at[src], zb_s.at[0], zb_r.at[src], (src * NX + x, n)).wait_recv()
+
+    loop(0, N_CEN - 1, lc_wait)
+    l_tok[pl.ds(t, 1)] = lse(l_cen[...])[None]
+    loop(0, N_TOK - 1, lambda j: lt_copy(tok_of(j)).start())
 
     loop(1, NX, lambda k: xb_copy(k).wait_recv())
     rows = xb_out[pl.ds(x, 1)][0].astype(jnp.float32)
@@ -322,9 +343,9 @@
     yb_out[...] = rows.astype(jnp.bfloat16)
     loop(1, NY, lambda k: yb_copy(k).start())
 
-    loop(0, N_CEN - 1, lc_wait)
-    l_tok[pl.ds(t, 1)] = lse(l_cen[...])[None]
-    loop(0, N_TOK - 1, lambda j: lt_copy(tok_of(j)).start())
+    loop(0, N_TOK - 1, lt_wait)
+    l_all[pl.ds(n, 1)] = lse(l_tok[...])[None]
+    loop(0, N_CEN - 1, lambda j: la_copy(cen_of(j)).start())
 
     loop(1, NY, lambda k: ya_copy(k).wait_recv())
     rows = ya_out[pl.ds(y, 1)][0].astype(jnp.float32)
@@ -358,25 +379,24 @@
 
     zb_each(lambda zt: zb_copy(zt).start())
 
-    loop(0, N_TOK - 1, lt_wait)
-    l_all[pl.ds(n, 1)] = lse(l_tok[...])[None]
-    loop(0, N_CEN - 1, lambda j: la_copy(cen_of(j)).start())
+    upper = lax.broadcasted_iota(jnp.int32, (WIDTH, CHUNK), 0) < 64
 
     def product(k):
         yy = (y + ring(k) + NY) % NY
-        rows = []
+        total = None
         for h in range(2):
             ch = 2 * yy + h
-            g_row = jnp.exp2(m_ref[pl.ds(ch, 1)][0] - l_all[pl.ds(ch, 1)][0])
-            for b in range(2):
-                g = jnp.transpose(jnp.broadcast_to(g_row[:, b * ROWS : (b + 1) * ROWS], (WIDTH, ROWS)))
-                g_hi = g.astype(jnp.bfloat16).astype(jnp.float32)
-                tk = tok_all[pl.ds(2 * ch + b, 1)][0].astype(jnp.float32)
-                rows.append(
-                    jnp.concatenate([tk * g, jnp.where(lane < 64, g_hi, g - g_hi)], axis=1).astype(jnp.bfloat16)
-                )
-        e = e_ref[:, pl.ds(pl.multiple_of(yy * 2 * CHUNK, 2 * CHUNK), 2 * CHUNK)]
-        return jnp.dot(e, jnp.concatenate(rows, axis=0), preferred_element_type=jnp.float32)
+            g = jnp.exp2(m_ref[pl.ds(ch, 1)][0] - l_all[pl.ds(ch, 1)][0])
+            g_hi = g.astype(jnp.bfloat16).astype(jnp.float32)
+            top = tok_t[pl.ds(ch, 1)][0].astype(jnp.float32) * g
+            low = jnp.where(upper, g_hi, g - g_hi)
+            e = e_ref[:, pl.ds(pl.multiple_of(ch * CHUNK, CHUNK), CHUNK)]
+            out = lax.dot_general(
+                e, jnp.concatenate([top, low], axis=0).astype(jnp.bfloat16),
+                (((1,), (1,)), ((), ())), preferred_element_type=jnp.float32,
+            )
+            total = out if total is None else total + out
+        return total
 
     for group in ((0,), (1, 2), (3, 4), (5, 6, 7)):
         for k in group:
@@ -472,7 +492,8 @@
             vmem((N_TOK, 1, ROWS), jnp.int32),
             vmem((2, LOCAL, WIDTH), bf),
             vmem((LOCAL // ROWS, ROWS), f32),
-            vmem((LOCAL, 2 * WIDTH), bf),
+            vmem((LOCAL + WIDTH, 2 * WIDTH), bf),
+            vmem((N_CEN, WIDTH, CHUNK), bf),
             vmem((LOCAL, N_TOK * ROWS), bf),
             vmem((LOCAL, 2 * WIDTH), f32),
             vmem((N_CEN, 1, CHUNK), f32),

time: 63.6 us -> 58.7 us (0.923)
  Pallas kernels: 62.8 us -> 57.9 us
    pallas_call x1, Pallas kernels: 61.2 us -> 56.2 us  [per_device(): pl.pallas_call(kernel, out_shape=(jax.ShapeDtypeStruct((LOCAL, WIDTH), bf...]
where the time goes in v3:
time: 58.7 us; the launch traced here: 58.5 us
  Pallas kernels  57.9 us (99%)
  between operations  0.64 us (1%)
    pallas_call x1, Pallas kernels, per_device(): pl.pallas_call(kernel, out_shape=(jax.ShapeDtypeStruct((LOCAL, WIDTH), bf...  56.2 us
    pallas_call x1, Pallas kernels, per_device(): pl.pallas_call(hand_on, out_shape=tuple((jax.ShapeDtypeStruct(v.shape, v....  1.68 us

profile of v3, /device:TPU:1, one launch (start us, length us, event | category | flops | bytes accessed | tf_op | source)
XLA Modules:
  0.0 58.5 jit_solution(7224010185303222682)
XLA Ops:
  0.6 56.2 %shard_map.67 = (bf16[1024,128]{1,0:T(8,128)(2,1)}, f32[1,128]{1,0:T(1,128)}, bf16[8,128]{1,0:T(8,128)(2,1)}) custom-call(bf16[128,128]{1,0:T(8,128)(2,1)} %tok_hbm.1, s32[1,128]{1,0:T(1,128)} %bitcast.4, bf16[1024,128]{1,0:T(8,128)(2,1)} %cen_hbm.1, f32[8,128]{1,0:T(8,128)} %bitcast.3), custom_call_target="tpu_custom_call" | custom-call | tf_op jit(solution)/shard_map/pallas_call | solution.py:481
  56.9 1.7 %shard_map.68 = (bf16[1024,128]{1,0:T(8,128)(2,1)}, f32[1,128]{1,0:T(1,128)}, bf16[8,128]{1,0:T(8,128)(2,1)}) custom-call(bf16[1024,128]{1,0:T(8,128)(2,1)} %get-tuple-element.9.upd_in, f32[1,128]{1,0:T(1,128)} %get-tuple-element.10.norm_in, bf16[8,128]{1,0:T(8,128)(2,1)} %get-tuple-element.11.res_in), custom_call_target="tpu_custom_call" | custom-call | tf_op jit(solution)/shard_map/pallas_call | solution.py:521

commit v4 on v3

--- a/solution.py
+++ b/solution.py
@@ -18,11 +18,24 @@
 LN2 = math.log(2.0)
 VMEM_LIMIT = 60 << 20
 PICK_B, PICK_A = 8, 8
+SPLIT = 1
+
+
+def div(a, b):
+    return a // b if isinstance(a, int) else lax.div(a, b)
+
+
+def rem(a, b):
+    return a % b if isinstance(a, int) else lax.rem(a, b)
 
 
 def ring(s):
-    half = (s + 1) // 2
-    return half * (2 * (s % 2) - 1)
+    return div(s + 1, 2) * (2 * rem(s, 2) - 1)
+
+
+def place(d):
+    far = div(d, 5)
+    return (1 - far) * (2 * d - div(d + 7, 8)) + far * (16 - 2 * d)
 
 
 def loop(lo, hi, body):
@@ -33,6 +46,11 @@
     lax.fori_loop(lo, hi, step, 0)
 
 
+def each(lo, hi, body):
+    for i in range(lo, hi):
+        body(i)
+
+
 def split3(v):
     hi = v.astype(jnp.bfloat16).astype(jnp.float32)
     mid = (v - hi).astype(jnp.bfloat16).astype(jnp.float32)
@@ -41,26 +59,26 @@
 
 def kernel(
     tok_hbm, ids_hbm, cen_hbm, lp_hbm, upd_ref, norm_ref, res_ref,
-    tok_all, ids_all, cen2, lp_ref, cen_aug, tok_t, e_ref, acc, m_ref, l_send, l_cen, l_tok, l_all,
+    tok_all, ids_all, cen2, lp_ref, cen_aug, tok_t, e_ref, g_ref, acc, m_ref, l_send, l_cen, l_tok, l_all,
     cols, ya_out, ya_in, ta_out, ta_in, xb_out, xb_in, yb_out, yb_in, zb_out, zb_in, tok_f32,
     in_s, z_s, z_r, x_s, x_r, f_s, f_r, idz_s, idz_r, idx_s, idx_r, cen_s, cen_r,
     lc_s, lc_r, lt_s, lt_r, la_s, la_r, ya_s, ya_r, ta_s, ta_r, xb_s, xb_r, yb_s, yb_r, zb_s, zb_r,
 ):
     t = lax.axis_index("tok")
     n = lax.axis_index("cen")
-    x, z = t % NX, t // NX
-    y, c = n // 2, n % 2
+    x, z = rem(t, NX), div(t, NX)
+    y, c = div(n, 2), rem(n, 2)
     sib = (t, y * 2 + 1 - c)
     unit = math.log2(math.e) / math.sqrt(WIDTH)
 
     def at_x(k):
-        return (z * NX + (x + k) % NX, n)
+        return (z * NX + rem(x + k, NX), n)
 
     def at_y(k):
-        return (t, ((y + k) % NY) * 2 + c)
+        return (t, rem(y + k, NY) * 2 + c)
 
     def at_z(k):
-        return (((z + k) % NZ) * NX + x, n)
+        return (rem(z + k, NZ) * NX + x, n)
 
     def copy(src, dst, send, recv, dev):
         return pltpu.make_async_remote_copy(
@@ -72,9 +90,9 @@
     def greet(dev):
         pl.semaphore_signal(barrier, inc=1, device_id=dev, device_id_type=MESH)
 
-    loop(1, NZ, lambda k: greet(at_z(k)))
-    loop(1, NY, lambda k: greet(at_y(k)))
-    loop(1, NX, lambda k: greet(at_x(k)))
+    each(1, NZ, lambda k: greet(at_z(k)))
+    each(1, NY, lambda k: greet(at_y(k)))
+    each(1, NX, lambda k: greet(at_x(k)))
     greet(sib)
 
     fetch = [
@@ -115,7 +133,7 @@
         return copy(tok_all.at[t], tok_all.at[t], z_s.at[s], z_r.at[s], at_z(NZ - ring(s)))
 
     def block(s, k):
-        return ((z + ring(s) + NZ) % NZ) * NX + (x + k) % NX
+        return rem(z + ring(s) + NZ, NZ) * NX + rem(x + k, NX)
 
     def x_copy(s, k):
         b = block(s, 0)
@@ -126,10 +144,10 @@
         return copy(tok_all.at[b], tok_all.at[b], f_s.at[s, k], f_r.at[s, k], sib)
 
     def if_mine(s, core, todo):
-        pl.when(s % 2 == core)(todo)
-
-    loop(1, NZ, lambda k: idz_copy(k).start())
-    loop(1, NZ, lambda s: if_mine(s, c, lambda: z_copy(s).start()))
+        pl.when(rem(s, 2) == core)(todo)
+
+    each(1, NZ, lambda k: idz_copy(k).start())
+    each(1, NZ, lambda s: if_mine(s, c, lambda: z_copy(s).start()))
     cen_copy().start()
 
     def receive_z(s):
@@ -170,7 +188,8 @@
                 f_copy(s, k).wait_recv()
 
         if_mine(s, 1 - c, todo)
-        zz = (z + ring(s) + NZ) % NZ
+        zz = rem(z + ring(s) + NZ, NZ)
+        spot = place(rem(zz - y + NY, NY))
         parts = []
         for h in range(2):
             ch = 2 * zz + h
@@ -183,7 +202,7 @@
             raw = raw[:LOCAL]
             top = jnp.max(raw, axis=0, keepdims=True)
             e = jnp.exp2((raw - top) * unit)
-            e_ref[:, pl.ds(pl.multiple_of(ch * CHUNK, CHUNK), CHUNK)] = e.astype(jnp.bfloat16)
+            e_ref[:, pl.ds(pl.multiple_of((2 * spot + h) * CHUNK, CHUNK), CHUNK)] = e.astype(jnp.bfloat16)
             total = jnp.sum(e, axis=0, keepdims=True)
             m_ref[pl.ds(ch, 1)] = (top * unit)[None]
             part = top * unit + jnp.log2(total)
@@ -202,16 +221,16 @@
                 l_cen[pl.ds(ch, 1)] = part[None]
 
     def ya_copy(k):
-        return copy(ya_out.at[(y + k) % NY], ya_in.at[k], ya_s.at[k], ya_r.at[k], at_y(k))
+        return copy(ya_out.at[rem(y + k, NY)], ya_in.at[k], ya_s.at[k], ya_r.at[k], at_y(k))
 
     def xb_copy(k):
-        return copy(xb_out.at[(x + k) % NX], xb_in.at[k], xb_s.at[k], xb_r.at[k], at_x(k))
+        return copy(xb_out.at[rem(x + k, NX)], xb_in.at[k], xb_s.at[k], xb_r.at[k], at_x(k))
 
     def yb_copy(k):
-        return copy(yb_out.at[(y + k) % NY], yb_in.at[k], yb_s.at[k], yb_r.at[k], at_y(k))
+        return copy(yb_out.at[rem(y + k, NY)], yb_in.at[k], yb_s.at[k], yb_r.at[k], at_y(k))
 
     def pick_prepare():
-        loop(1, NX, lambda k: idx_copy(k).wait_recv())
+        each(1, NX, lambda k: idx_copy(k).wait_recv())
         first = (t * N_CEN + y * 2) * LOCAL
         rel = (ids_all[...].reshape(N_TOK, ROWS) - first).astype(jnp.float32)
         rel = jnp.transpose(rel).reshape(NY, 2, 8, N_TOK)
@@ -250,29 +269,29 @@
 
     def pick_a():
         loop(0, 2, part_a)
-        loop(1, NY, lambda k: ya_copy(k).start())
+        each(1, NY, lambda k: ya_copy(k).start())
 
     def pick_b():
         pick_prepare()
         loop(2, 4, part_b)
-        loop(1, NX, lambda k: xb_copy(k).start())
+        each(1, NX, lambda k: xb_copy(k).start())
 
     def ids_along_x():
-        loop(1, NZ, lambda k: idz_copy(k).wait_recv())
-        loop(1, NX, lambda k: idx_copy(k).start())
+        each(1, NZ, lambda k: idz_copy(k).wait_recv())
+        each(1, NX, lambda k: idx_copy(k).start())
 
     receive_z(0)
     cen_copy().wait_recv()
-    loop(1, 3, receive_z)
+    each(1, 3, receive_z)
     receive_x(0)
-    loop(3, 5, receive_z)
+    each(3, 5, receive_z)
     ids_along_x()
 
     def step(s):
         @pl.when(s == 1)
         def _():
-            loop(5, NZ, receive_z)
-            loop(1, 3, receive_x)
+            each(5, NZ, receive_z)
+            each(1, 3, receive_x)
 
         @pl.when((s >= 1) & (s + 2 < NZ))
         def _():
@@ -291,10 +310,10 @@
         pick_a()
 
     def tok_of(j):
-        return ((z + ring(7 - j // NX) + NZ) % NZ) * NX + (x + 1 + j % NX) % NX
+        return rem(z + ring(7 - div(j, NX)) + NZ, NZ) * NX + rem(x + 1 + rem(j, NX), NX)
 
     def cen_of(j):
-        return ((y + ring(7 - j // 2) + NY) % NY) * 2 + (c + 1 + j) % 2
+        return rem(y + ring(7 - div(j, 2)) + NY, NY) * 2 + rem(c + 1 + rem(j, 2), 2)
 
     def lse(v):
         top = jnp.max(v, axis=0)
@@ -332,22 +351,39 @@
     def zb_wait(src):
         copy(zb_out.at[0], zb_in.at[src], zb_s.at[0], zb_r.at[src], (src * NX + x, n)).wait_recv()
 
-    loop(0, N_CEN - 1, lc_wait)
+    each(0, N_CEN - 1, lc_wait)
     l_tok[pl.ds(t, 1)] = lse(l_cen[...])[None]
-    loop(0, N_TOK - 1, lambda j: lt_copy(tok_of(j)).start())
-
-    loop(1, NX, lambda k: xb_copy(k).wait_recv())
+    each(0, N_TOK - 1, lambda j: lt_copy(tok_of(j)).start())
+
+    each(1, NX, lambda k: xb_copy(k).wait_recv())
     rows = xb_out[pl.ds(x, 1)][0].astype(jnp.float32)
     for k in range(1, NX):
         rows = rows + xb_in[k].astype(jnp.float32)
     yb_out[...] = rows.astype(jnp.bfloat16)
-    loop(1, NY, lambda k: yb_copy(k).start())
-
-    loop(0, N_TOK - 1, lt_wait)
+    each(1, NY, lambda k: yb_copy(k).start())
+
+    def sent(s):
+        def todo():
+            if s > 0:
+                z_copy(s).wait_send()
+                f_copy(s, 0).wait_send()
+            for k in range(1, NX):
+                x_copy(s, k).wait_send()
+                f_copy(s, k).wait_send()
+
+        if_mine(s, c, todo)
+
+    each(0, NZ, sent)
+    cen_copy().wait_send()
+    each(1, NZ, lambda k: idz_copy(k).wait_send())
+    each(1, NX, lambda k: idx_copy(k).wait_send())
+    each(0, N_CEN - 1, lambda j: lc_copy(cen_of(j)).wait_send())
+
+    each(0, N_TOK - 1, lt_wait)
     l_all[pl.ds(n, 1)] = lse(l_tok[...])[None]
-    loop(0, N_CEN - 1, lambda j: la_copy(cen_of(j)).start())
-
-    loop(1, NY, lambda k: ya_copy(k).wait_recv())
+    each(0, N_CEN - 1, lambda j: la_copy(cen_of(j)).start())
+
+    each(1, NY, lambda k: ya_copy(k).wait_recv())
     rows = ya_out[pl.ds(y, 1)][0].astype(jnp.float32)
     for k in range(1, NY):
         rows = rows + ya_in[k].astype(jnp.float32)
@@ -359,11 +395,11 @@
             def _():
                 act(to)
 
-        loop(0, half * NX, body)
+        each(0, half * NX, body)
 
     ta_each(lambda to: ta_copy(to).start())
 
-    loop(1, NY, lambda k: yb_copy(k).wait_recv())
+    each(1, NY, lambda k: yb_copy(k).wait_recv())
     rows = yb_out[pl.ds(y, 1)][0].astype(jnp.float32)
     for k in range(1, NY):
         rows = rows + yb_in[k].astype(jnp.float32)
@@ -375,97 +411,68 @@
             def _():
                 act(zt)
 
-        loop(half, NZ, body)
+        each(half, NZ, body)
 
     zb_each(lambda zt: zb_copy(zt).start())
 
+    each(1, NX, lambda k: xb_copy(k).wait_send())
+    each(1, NY, lambda k: ya_copy(k).wait_send())
+    each(0, N_TOK - 1, lambda j: lt_copy(tok_of(j)).wait_send())
+
     upper = lax.broadcasted_iota(jnp.int32, (WIDTH, CHUNK), 0) < 64
 
-    def product(k):
-        yy = (y + ring(k) + NY) % NY
-        total = None
+    def scale(k):
+        yy = rem(y + ring(k) + NY, NY)
         for h in range(2):
             ch = 2 * yy + h
+
+            @pl.when(ch != n)
+            def _():
+                la_wait(ch)
+
             g = jnp.exp2(m_ref[pl.ds(ch, 1)][0] - l_all[pl.ds(ch, 1)][0])
             g_hi = g.astype(jnp.bfloat16).astype(jnp.float32)
             top = tok_t[pl.ds(ch, 1)][0].astype(jnp.float32) * g
             low = jnp.where(upper, g_hi, g - g_hi)
-            e = e_ref[:, pl.ds(pl.multiple_of(ch * CHUNK, CHUNK), CHUNK)]
-            out = lax.dot_general(
-                e, jnp.concatenate([top, low], axis=0).astype(jnp.bfloat16),
-                (((1,), (1,)), ((), ())), preferred_element_type=jnp.float32,
-            )
-            total = out if total is None else total + out
-        return total
-
-    for group in ((0,), (1, 2), (3, 4), (5, 6, 7)):
-        for k in group:
-            for h in range(2):
-                ch = 2 * ((y + ring(k) + NY) % NY) + h
-
-                @pl.when(ch != n)
-                def _():
-                    la_wait(ch)
-
-        for k in group:
-            if k == 0:
-                acc[...] = product(k)
-            else:
-                acc[...] += product(k)
+            at = (2 * k + h) * CHUNK
+            g_ref[:WIDTH, at : at + CHUNK] = top.astype(jnp.bfloat16)
+            g_ref[WIDTH:, at : at + CHUNK] = low.astype(jnp.bfloat16)
+
+    def product(lo, hi):
+        at = slice(lo * 2 * CHUNK, hi * 2 * CHUNK)
+        return lax.dot_general(
+            e_ref[:, at], g_ref[:, at], (((1,), (1,)), ((), ())), preferred_element_type=jnp.float32
+        )
+
+    for k in range(SPLIT):
+        scale(k)
+    acc[...] = product(0, SPLIT)
+    for k in range(SPLIT, NY):
+        scale(k)
+    acc[...] += product(SPLIT, NY)
     mass = acc[:, WIDTH:]
     mass = mass + pltpu.roll(mass, 64, 1)
     upd_ref[...] = (acc[:, :WIDTH] / mass).astype(jnp.bfloat16)
 
-    own = l_all[pl.ds(t // 2, 1)][0] * LN2
-    norm_ref[...] = jnp.where(t % 2 == 0, own[:, :ROWS], own[:, ROWS:])
+    own = l_all[pl.ds(div(t, 2), 1)][0] * LN2
+    norm_ref[...] = jnp.where(rem(t, 2) == 0, own[:, :ROWS], own[:, ROWS:])
 
     mine = tok_f32[pl.ds(pl.multiple_of(n * 8, 8), 8), :]
 
     @pl.when(z < half)
     def _():
         ta_in[pl.ds(t, 1)] = ta_out[pl.ds(t, 1)]
-        loop(0, N_TOK - 1, lambda j: ta_wait(tok_of(j)))
+        each(0, N_TOK - 1, lambda j: ta_wait(tok_of(j)))
         res_ref[...] = (mine - jnp.sum(ta_in[...], axis=0)).astype(jnp.bfloat16)
 
     @pl.when(z >= half)
     def _():
         zb_in[pl.ds(z, 1)] = zb_out[pl.ds(z - half, 1)]
-        loop(1, NZ, lambda k: zb_wait((z + k) % NZ))
+        each(1, NZ, lambda k: zb_wait(rem(z + k, NZ)))
         res_ref[...] = (mine - jnp.sum(zb_in[...], axis=0)).astype(jnp.bfloat16)
 
-    def sent(s):
-        def todo():
-            @pl.when(s > 0)
-            def _():
-                z_copy(s).wait_send()
-                f_copy(s, 0).wait_send()
-
-            for k in range(1, NX):
-                x_copy(s, k).wait_send()
-                f_copy(s, k).wait_send()
-
-        if_mine(s, c, todo)
-
-    loop(0, NZ, sent)
-    cen_copy().wait_send()
-
-    def sent_axis(k):
-        idz_copy(k).wait_send()
-        ya_copy(k).wait_send()
-        yb_copy(k).wait_send()
-
-    def sent_x(k):
-        idx_copy(k).wait_send()
-        xb_copy(k).wait_send()
-
-    def sent_cen(j):
-        lc_copy(cen_of(j)).wait_send()
-        la_copy(cen_of(j)).wait_send()
-
-    loop(1, NZ, sent_axis)
-    loop(1, NX, sent_x)
-    loop(0, N_CEN - 1, sent_cen)
-    loop(0, N_TOK - 1, lambda j: lt_copy(tok_of(j)).wait_send())
+    each(1, NY, lambda k: yb_copy(k).wait_send())
+    each(0, N_CEN - 1, lambda j: la_copy(cen_of(j)).wait_send())
     ta_each(lambda to: ta_copy(to).wait_send())
     zb_each(lambda zt: zb_copy(zt).wait_send())
 
@@ -495,6 +502,7 @@
             vmem((LOCAL + WIDTH, 2 * WIDTH), bf),
             vmem((N_CEN, WIDTH, CHUNK), bf),
             vmem((LOCAL, N_TOK * ROWS), bf),
+            vmem((2 * WIDTH, N_TOK * ROWS), bf),
             vmem((LOCAL, 2 * WIDTH), f32),
             vmem((N_CEN, 1, CHUNK), f32),
             vmem((N_CEN, 1, CHUNK), f32),

time: 58.7 us -> 55.9 us (0.952)
  Pallas kernels: 57.9 us -> 54.9 us
    pallas_call x1, Pallas kernels: 56.2 us -> 53.2 us  [per_device(): pl.pallas_call(kernel, out_shape=(jax.ShapeDtypeStruct((LOCAL, WIDTH), bf...]
where the time goes in v4:
time: 55.9 us; the launch traced here: 55.5 us
  Pallas kernels  54.9 us (98%)
  between operations  0.64 us (1%)
    pallas_call x1, Pallas kernels, per_device(): pl.pallas_call(kernel, out_shape=(jax.ShapeDtypeStruct((LOCAL, WIDTH), bf...  53.2 us
    pallas_call x1, Pallas kernels, per_device(): pl.pallas_call(hand_on, out_shape=tuple((jax.ShapeDtypeStruct(v.shape, v....  1.68 us

profile of v4, /device:TPU:1, one launch (start us, length us, event | category | flops | bytes accessed | tf_op | source)
XLA Modules:
  0.0 55.5 jit_solution(12441879195856609029)
XLA Ops:
  0.6 53.2 %shard_map.67 = (bf16[1024,128]{1,0:T(8,128)(2,1)}, f32[1,128]{1,0:T(1,128)}, bf16[8,128]{1,0:T(8,128)(2,1)}) custom-call(bf16[128,128]{1,0:T(8,128)(2,1)} %tok_hbm.1, s32[1,128]{1,0:T(1,128)} %bitcast.4, bf16[1024,128]{1,0:T(8,128)(2,1)} %cen_hbm.1, f32[8,128]{1,0:T(8,128)} %bitcast.3), custom_call_target="tpu_custom_call" | custom-call | tf_op jit(solution)/shard_map/pallas_call | solution.py:488
  53.8 1.7 %shard_map.68 = (bf16[1024,128]{1,0:T(8,128)(2,1)}, f32[1,128]{1,0:T(1,128)}, bf16[8,128]{1,0:T(8,128)(2,1)}) custom-call(bf16[1024,128]{1,0:T(8,128)(2,1)} %get-tuple-element.9.upd_in, f32[1,128]{1,0:T(1,128)} %get-tuple-element.10.norm_in, bf16[8,128]{1,0:T(8,128)(2,1)} %get-tuple-element.11.res_in), custom_call_target="tpu_custom_call" | custom-call | tf_op jit(solution)/shard_map/pallas_call | solution.py:529

commit v5 on v4

--- a/solution.py
+++ b/solution.py
@@ -273,6 +273,9 @@
 
     def pick_b():
         pick_prepare()
+        pick_b2()
+
+    def pick_b2():
         loop(2, 4, part_b)
         each(1, NX, lambda k: xb_copy(k).start())
 
@@ -304,10 +307,9 @@
         score(s)
 
     loop(0, NZ, step)
-    if PICK_B >= NZ:
-        pick_b()
-    if PICK_A >= NZ:
-        pick_a()
+    pick_prepare()
+    pick_a()
+    pick_b2()
 
     def tok_of(j):
         return rem(z + ring(7 - div(j, NX)) + NZ, NZ) * NX + rem(x + 1 + rem(j, NX), NX)

time: 55.9 us -> 54.6 us (0.977)
  Pallas kernels: 54.9 us -> 53.8 us
    pallas_call x1, Pallas kernels: 53.2 us -> 52.1 us  [per_device(): pl.pallas_call(kernel, out_shape=(jax.ShapeDtypeStruct((LOCAL, WIDTH), bf...]
where the time goes in v5:
time: 54.6 us; the launch traced here: 54.5 us
  Pallas kernels  53.8 us (99%)
  between operations  0.64 us (1%)
    pallas_call x1, Pallas kernels, per_device(): pl.pallas_call(kernel, out_shape=(jax.ShapeDtypeStruct((LOCAL, WIDTH), bf...  52.1 us
    pallas_call x1, Pallas kernels, per_device(): pl.pallas_call(hand_on, out_shape=tuple((jax.ShapeDtypeStruct(v.shape, v....  1.68 us

profile of v5, /device:TPU:1, one launch (start us, length us, event | category | flops | bytes accessed | tf_op | source)
XLA Modules:
  0.0 54.5 jit_solution(881413803254499029)
XLA Ops:
  0.6 52.1 %shard_map.67 = (bf16[1024,128]{1,0:T(8,128)(2,1)}, f32[1,128]{1,0:T(1,128)}, bf16[8,128]{1,0:T(8,128)(2,1)}) custom-call(bf16[128,128]{1,0:T(8,128)(2,1)} %tok_hbm.1, s32[1,128]{1,0:T(1,128)} %bitcast.4, bf16[1024,128]{1,0:T(8,128)(2,1)} %cen_hbm.1, f32[8,128]{1,0:T(8,128)} %bitcast.3), custom_call_target="tpu_custom_call" | custom-call | tf_op jit(solution)/shard_map/pallas_call | solution.py:490
  52.8 1.7 %shard_map.68 = (bf16[1024,128]{1,0:T(8,128)(2,1)}, f32[1,128]{1,0:T(1,128)}, bf16[8,128]{1,0:T(8,128)(2,1)}) custom-call(bf16[1024,128]{1,0:T(8,128)(2,1)} %get-tuple-element.9.upd_in, f32[1,128]{1,0:T(1,128)} %get-tuple-element.10.norm_in, bf16[8,128]{1,0:T(8,128)(2,1)} %get-tuple-element.11.res_in), custom_call_target="tpu_custom_call" | custom-call | tf_op jit(solution)/shard_map/pallas_call | solution.py:531
